TPU v7x, 256 devices: a whole 4x4x8 slice. The times are simulated.
256 devices in a mesh: fluid: 64 (over x, z, core), metal: 4 (over y).
Axes of the slice: x: 4, y: 4, z: 8, core: 2. Of those that a mesh axis runs over, the one named last changes fastest.
Arguments:
- fluid_x: bfloat16 [16384, 512], P('fluid', 'metal'), may hold values from -32 to 32
- metal_x: bfloat16 [8192, 512], P('fluid', 'metal'), may hold values from -32 to 32
- w_rf: bfloat16 [512, 512], P(None, 'metal'), may hold values from -0.5 to 0.5
- w_vf: bfloat16 [512, 512], P(None, 'metal'), may hold values from -0.25 to 0.25
- w_rm: bfloat16 [512, 512], P(None, 'metal'), may hold values from -0.5 to 0.5
- w_vm: bfloat16 [512, 512], P(None, 'metal'), may hold values from -0.25 to 0.25
- fluid_grad: bfloat16 [16384, 512], P('fluid', 'metal'), may hold values from -6 to 6
- metal_grad: bfloat16 [8192, 512], P('fluid', 'metal'), may hold values from -6 to 6
- pair_list: int32 [2048, 2], P('fluid'), may hold values from 0 to 63, as said below
- pair_count: int32 [64], P('fluid'), may hold values from 2 to 32, as said below
Outputs:
- fluid_out: bfloat16 [16384, 512], P('fluid', 'metal')
- metal_out: bfloat16 [8192, 512], P('fluid', 'metal')
- fluid_dx: bfloat16 [16384, 512], P('fluid', 'metal')
- metal_dx: bfloat16 [8192, 512], P('fluid', 'metal')
- weight_grads: float32 [4, 512, 512], P(None, None, 'metal')
Inputs may be any that keep to these rules, and one draw needn't show every extreme that they name: `pair_list`: column 0 is a local fluid block below 2, column 1 a metal block below 64. The first pair_count[d] entries of fluid index d are distinct pairs; every fluid block of every index and every metal block stands in some live entry; entries past the count hold valid indices and are ignored. `pair_count`: some fluid index has all 32 slots live.
All inputs are finite; a program needn't handle non-finite values.
Results may differ from a plain program's by a relative error of at most 0.0179.
The roundings to bfloat16 on the way count: a program that leaves them out, or rounds other values in their place, can miss the bound.
Values may be sent and summed in bfloat16 or wider, within the bound.
No kernel may reach another device: no remote copies, remote signals or barrier semaphores. Data moves between devices by JAX's collectives and lax.ppermute only.
A program may use at most 128 MiB of HBM per device.

v0:
```python
import math
import jax
import jax.numpy as jnp
from jax import lax
from jax.sharding import PartitionSpec as P

D = 512
H = 8
BLK = 128
LOWEST = -1e30


def project(inputs, weight):
    return jnp.dot(inputs, weight, preferred_element_type=jnp.float32).astype(jnp.bfloat16)


def back_project(grads, weight):
    return lax.dot_general(
        grads, weight, (((1,), (1,)), ((), ())), preferred_element_type=jnp.float32
    )


def outer_rows(inputs, grads):
    return lax.dot_general(
        inputs, grads, (((0,), (0,)), ((), ())), preferred_element_type=jnp.float32
    )


def body(fluid_x, metal_x, w_rf, w_vf, w_rm, w_vm, fluid_grad, metal_grad, pair_list, pair_count):
    head_size = D // H
    local_heads = w_rf.shape[1] // head_size
    feature_cols = w_rf.shape[1]
    fluid_rows = fluid_x.shape[0]
    blocks = fluid_rows // BLK
    metal_blocks = lax.axis_size("fluid")
    metal_rows = metal_blocks * BLK
    slot_total = pair_list.shape[0]
    batch_size = math.gcd(slot_total, 16)
    inv_root = 1.0 / math.sqrt(head_size)
    live_count = pair_count[0]
    loop_turns = slot_total // batch_size
    fluid_full, metal_full = (
        lax.all_gather(fluid_x, "metal", axis=1, tiled=True),
        lax.all_gather(metal_x, "metal", axis=1, tiled=True),
    )
    fluid_keys = project(fluid_full, w_rf)
    fluid_values = project(fluid_full, w_vf)
    metal_keys = project(metal_full, w_rm)
    metal_values = project(metal_full, w_vm)
    keys_all, values_all = (
        lax.all_gather(metal_keys, "fluid", axis=0, tiled=True),
        lax.all_gather(metal_values, "fluid", axis=0, tiled=True),
    )
    fkey_tiles = fluid_keys.reshape(blocks, BLK, local_heads, head_size)
    fval_tiles = fluid_values.reshape(blocks, BLK, local_heads, head_size)
    mkey_tiles = keys_all.reshape(metal_blocks, BLK, local_heads, head_size)
    mval_tiles = values_all.reshape(metal_blocks, BLK, local_heads, head_size)

    def batch_pairs(number):
        entries = lax.dynamic_slice_in_dim(pair_list, number * batch_size, batch_size, 0)
        slot_index = number * batch_size + jnp.arange(batch_size, dtype=jnp.int32)
        frows = entries[:, 0]
        mrows = entries[:, 1]
        scores = (
            jnp.einsum(
                "pahd,pbhd->phab",
                fkey_tiles[frows],
                mkey_tiles[mrows],
                preferred_element_type=jnp.float32,
            )
            * inv_root
        )
        return (frows, mrows, slot_index < live_count, scores)

    def max_pass(number, state):
        row_max, col_max = state
        frows, mrows, active, scores = batch_pairs(number)
        live = active[:, None, None]
        row_max = row_max.at[frows].max(jnp.where(live, jnp.max(scores, axis=3), LOWEST))
        col_max = col_max.at[mrows].max(jnp.where(live, jnp.max(scores, axis=2), LOWEST))
        return (row_max, col_max)

    row_max, col_local = lax.fori_loop(
        0,
        loop_turns,
        max_pass,
        (
            jnp.full((blocks, local_heads, BLK), LOWEST, jnp.float32),
            jnp.full((metal_blocks, local_heads, BLK), LOWEST, jnp.float32),
        ),
    )
    col_max = lax.pmax(col_local, "fluid")

    def sum_pass(number, state):
        row_sum, fluid_num, col_sum, metal_num = state
        frows, mrows, active, scores = batch_pairs(number)
        live = active[:, None, None, None]
        row_exp = jnp.where(live, jnp.exp(scores - row_max[frows][:, :, :, None]), 0.0)
        col_exp = jnp.where(live, jnp.exp(scores - col_max[mrows][:, :, None, :]), 0.0)
        row_sum = row_sum.at[frows].add(jnp.sum(row_exp, axis=3))
        col_sum = col_sum.at[mrows].add(jnp.sum(col_exp, axis=2))
        fluid_num = fluid_num.at[frows].add(
            jnp.einsum(
                "phab,pbhd->pahd",
                row_exp.astype(jnp.bfloat16),
                mval_tiles[mrows],
                preferred_element_type=jnp.float32,
            )
        )
        metal_num = metal_num.at[mrows].add(
            jnp.einsum(
                "phab,pahd->pbhd",
                col_exp.astype(jnp.bfloat16),
                fval_tiles[frows],
                preferred_element_type=jnp.float32,
            )
        )
        return (row_sum, fluid_num, col_sum, metal_num)

    row_sum, fluid_num, col_sum, metal_num = lax.fori_loop(
        0,
        loop_turns,
        sum_pass,
        (
            jnp.zeros((blocks, local_heads, BLK), jnp.float32),
            jnp.zeros((blocks, BLK, local_heads, head_size), jnp.float32),
            jnp.zeros((metal_blocks, local_heads, BLK), jnp.float32),
            jnp.zeros((metal_blocks, BLK, local_heads, head_size), jnp.float32),
        ),
    )
    fluid_out = (
        (fluid_num / row_sum.transpose(0, 2, 1)[:, :, :, None])
        .reshape(fluid_rows, feature_cols)
        .astype(jnp.bfloat16)
    )
    num_rows = metal_num.reshape(metal_rows, feature_cols)
    total_rows = col_sum.transpose(0, 2, 1).reshape(metal_rows, local_heads)
    own_num, own_sum = (
        lax.psum_scatter(num_rows, "fluid", scatter_dimension=0, tiled=True),
        lax.psum_scatter(total_rows, "fluid", scatter_dimension=0, tiled=True),
    )
    metal_out = (
        (own_num.reshape(BLK, local_heads, head_size) / own_sum[:, :, None])
        .reshape(BLK, feature_cols)
        .astype(jnp.bfloat16)
    )
    scaled_grad = (
        (metal_grad.astype(jnp.float32).reshape(BLK, local_heads, head_size) / own_sum[:, :, None])
        .reshape(BLK, feature_cols)
        .astype(jnp.bfloat16)
    )
    scaled_all, output_all = (
        lax.all_gather(scaled_grad, "fluid", axis=0, tiled=True),
        lax.all_gather(metal_out, "fluid", axis=0, tiled=True),
    )
    delta_f = jnp.sum(
        (fluid_grad.astype(jnp.float32) * fluid_out.astype(jnp.float32)).reshape(
            fluid_rows, local_heads, head_size
        ),
        axis=2,
    )
    delta_m = jnp.sum(
        (scaled_all.astype(jnp.float32) * output_all.astype(jnp.float32)).reshape(
            metal_blocks, BLK, local_heads, head_size
        ),
        axis=3,
    )
    grad_tiles = fluid_grad.reshape(blocks, BLK, local_heads, head_size)
    scaled_tiles = scaled_all.reshape(metal_blocks, BLK, local_heads, head_size)
    dfluid_tiles = delta_f.reshape(blocks, BLK, local_heads)

    def grad_pass(number, state):
        grad_rf, grad_vf, grad_rm, grad_vm = state
        frows, mrows, active, scores = batch_pairs(number)
        live = active[:, None, None, None]
        attn = jnp.where(
            live,
            jnp.exp(scores - row_max[frows][:, :, :, None]) / row_sum[frows][:, :, :, None],
            0.0,
        )
        col_exp = jnp.where(live, jnp.exp(scores - col_max[mrows][:, :, None, :]), 0.0)
        fluid_term = jnp.einsum(
            "pahd,pbhd->phab",
            grad_tiles[frows],
            mval_tiles[mrows],
            preferred_element_type=jnp.float32,
        )
        metal_term = jnp.einsum(
            "pahd,pbhd->phab",
            fval_tiles[frows],
            scaled_tiles[mrows],
            preferred_element_type=jnp.float32,
        )
        dscore = attn * (fluid_term - dfluid_tiles[frows].transpose(0, 2, 1)[:, :, :, None])
        dscore = dscore + col_exp * (metal_term - delta_m[mrows].transpose(0, 2, 1)[:, :, None, :])
        dscore_weight = dscore.astype(jnp.bfloat16)
        grad_rf = grad_rf.at[frows].add(
            jnp.einsum(
                "phab,pbhd->pahd",
                dscore_weight,
                mkey_tiles[mrows],
                preferred_element_type=jnp.float32,
            )
            * inv_root
        )
        grad_vf = grad_vf.at[frows].add(
            jnp.einsum(
                "phab,pbhd->pahd",
                col_exp.astype(jnp.bfloat16),
                scaled_tiles[mrows],
                preferred_element_type=jnp.float32,
            )
        )
        grad_rm = grad_rm.at[mrows].add(
            jnp.einsum(
                "phab,pahd->pbhd",
                dscore_weight,
                fkey_tiles[frows],
                preferred_element_type=jnp.float32,
            )
            * inv_root
        )
        grad_vm = grad_vm.at[mrows].add(
            jnp.einsum(
                "phab,pahd->pbhd",
                attn.astype(jnp.bfloat16),
                grad_tiles[frows],
                preferred_element_type=jnp.float32,
            )
        )
        return (grad_rf, grad_vf, grad_rm, grad_vm)

    grad_rf, grad_vf, grad_rm, grad_vm = lax.fori_loop(
        0,
        loop_turns,
        grad_pass,
        (
            jnp.zeros((blocks, BLK, local_heads, head_size), jnp.float32),
            jnp.zeros((blocks, BLK, local_heads, head_size), jnp.float32),
            jnp.zeros((metal_blocks, BLK, local_heads, head_size), jnp.float32),
            jnp.zeros((metal_blocks, BLK, local_heads, head_size), jnp.float32),
        ),
    )
    rf_rounded = grad_rf.reshape(fluid_rows, feature_cols).astype(jnp.bfloat16)
    vf_rounded = grad_vf.reshape(fluid_rows, feature_cols).astype(jnp.bfloat16)
    fluid_part = back_project(rf_rounded, w_rf) + back_project(vf_rounded, w_vf)
    fluid_part, weight_rf, weight_vf = (
        fluid_part,
        outer_rows(fluid_full, rf_rounded),
        outer_rows(fluid_full, vf_rounded),
    )
    rm_rounded = lax.psum_scatter(
        grad_rm.reshape(metal_rows, feature_cols), "fluid", scatter_dimension=0, tiled=True
    ).astype(jnp.bfloat16)
    vm_rounded = lax.psum_scatter(
        grad_vm.reshape(metal_rows, feature_cols), "fluid", scatter_dimension=0, tiled=True
    ).astype(jnp.bfloat16)
    metal_part = back_project(rm_rounded, w_rm) + back_project(vm_rounded, w_vm)
    weight_rm = outer_rows(metal_full, rm_rounded)
    weight_vm = outer_rows(metal_full, vm_rounded)
    fluid_dx, metal_dx = (
        lax.psum_scatter(fluid_part, "metal", scatter_dimension=1, tiled=True),
        lax.psum_scatter(metal_part, "metal", scatter_dimension=1, tiled=True),
    )
    weight_grads = lax.psum(jnp.stack([weight_rf, weight_vf, weight_rm, weight_vm]), "fluid")
    return (
        fluid_out,
        metal_out,
        fluid_dx.astype(jnp.bfloat16),
        metal_dx.astype(jnp.bfloat16),
        weight_grads,
    )


def solution(mesh):
    placed = (
        P("fluid", "metal"),
        P("fluid", "metal"),
        P(None, "metal"),
        P(None, "metal"),
        P(None, "metal"),
        P(None, "metal"),
        P("fluid", "metal"),
        P("fluid", "metal"),
        P("fluid", None),
        P("fluid"),
    )
    return jax.shard_map(
        body,
        mesh=mesh,
        in_specs=placed,
        out_specs=(
            P("fluid", "metal"),
            P("fluid", "metal"),
            P("fluid", "metal"),
            P("fluid", "metal"),
            P(None, None, "metal"),
        ),
        check_vma=False,
    )
```

profile of v0, /device:TPU:2, one launch (start us, length us, event | category | flops | bytes accessed | tf_op | source)
XLA Modules:
  0.0 1555.2 jit_solution(13822160661187020611)
XLA Ops:
  7.2 11.8 all_gather.19
  22.6 11.7 all_gather.18
  34.7 64.7 %all-gather.5.cloned.1.call-done = bf16[8192,128]{1,0:T(8,128)(2,1)} async-done(((bf16[128,128]{1,0:T(8,128)(2,1)}), bf16[8192,128]{1,0:T(8,128)(2,1)}) %all-gather.5.cloned.1.call-update) | async-done | bytes 2097168 | tf_op jit(solution)/shard_map/all_gather | solution.py:51
  99.4 8.2 reshape.334
  107.6 23.2 %while.53 = (s32[]{:T(128)}, f32[2,2,128]{2,1,0:T(2,128)S(1)}, f32[64,2,128]{2,1,0:T(2,128)S(1)}, s32[32,2]{0,1:T(2,128)S(1)}, s32[]{:T(128)}, /*index=5*/bf16[2...) while((s32[]{:T(128)}, f32[2,2,128]{2,1,0:T(2,128)S(1)}, ...), condition=%wide.region_5.6_spmd, body=%wide.region_0.5_spmd.sunk | while | flops 68692104 | bytes 3351623 | solution.py:83
  108.4 4.8 gather_fusion
  120.0 4.8 gather_fusion
  131.9 45.8 %all-gather.7.cloned.1.call-done = bf16[8192,128]{1,0:T(8,128)(2,1)} async-done(((bf16[128,128]{1,0:T(8,128)(2,1)}), bf16[8192,128]{1,0:T(8,128)(2,1)}) %all-gather.7.cloned.1.call-update) | async-done | bytes 2097168 | tf_op jit(solution)/shard_map/all_gather | solution.py:52
  177.7 8.3 reshape.335
  185.9 161.9 %all-reduce.3.cloned.1.call-done = f32[64,2,128]{2,1,0:T(2,128)} async-done(((f32[64,2,128]{2,1,0:T(2,128)}), f32[64,2,128]{2,1,0:T(2,128)}) %all-reduce.3.cloned.1.call-update) | async-done | bytes 65552 | tf_op jit(solution)/shard_map/pmax | solution.py:92
  350.3 67.5 %while.54 = (s32[]{:T(128)}, f32[2,2,128]{2,1,0:T(2,128)S(1)}, f32[2,128,2,64]{1,3,2,0:T(8,128)S(1)}, f32[64,2,128]{2,1,0:T(2,128)S(1)}, f32[64,128,2,64]{1,3,2,...) while((s32[]{:T(128)}, f32[2,2,128]{2,1,0:T(2,128)S(1)}, ...), condition=%wide.region_14.15_spmd, body=%wide.region_7.14_spmd.sunk | while | flops 209717376 | bytes 25437748 | solution.py:120
  353.3 4.8 gather_fusion.6
  358.2 5.7 gather_fusion.4
  386.7 4.8 gather_fusion.6
  391.6 5.7 gather_fusion.4
  425.2 5.2 copy.186
  431.3 130.0 %reduce-scatter.19.cloned.1.call-done = f32[128,2]{1,0:T(8,128)} async-done(((f32[8192,2]{1,0:T(8,128)}), f32[128,2]{1,0:T(8,128)}) %reduce-scatter.19.cloned.1.call-update) | async-done | bytes 1040
  562.2 145.2 %reduce-scatter.9.cloned.1.call-done = f32[128,128]{0,1:T(8,128)} async-done(((f32[8192,128]{0,1:T(8,128)}), f32[128,128]{0,1:T(8,128)}) %reduce-scatter.9.cloned.1.call-update) | async-done | bytes 65552 | tf_op jit(solution)/shard_map/reduce_scatter | solution.py:139
  710.1 72.3 %all-gather.9.cloned.1.call-done = bf16[8192,128]{0,1:T(8,128)(2,1)} async-done(((bf16[128,128]{0,1:T(8,128)(2,1)}), bf16[8192,128]{0,1:T(8,128)(2,1)}) %all-gather.9.cloned.1.call-update) | async-done | bytes 2097168 | tf_op jit(solution)/shard_map/all_gather | solution.py:153
  782.4 74.9 %all-gather.11.cloned.1.call-done = bf16[8192,128]{0,1:T(8,128)(2,1)} async-done(((bf16[128,128]{0,1:T(8,128)(2,1)}), bf16[8192,128]{0,1:T(8,128)(2,1)}) %all-gather.11.cloned.1.call-update) | async-done | bytes 2097168 | tf_op jit(solution)/shard_map/all_gather | solution.py:154
  867.4 5.2 copy.114
  877.5 131.7 %while.55 = (s32[]{:T(128)}, f32[2,128,2,64]{1,3,2,0:T(8,128)S(1)}, f32[2,128,2,64]{1,3,2,0:T(8,128)S(1)}, f32[64,128,2,64]{1,3,2,0:T(8,128)}, f32[64,128,2,64]{...) while((s32[]{:T(128)}, f32[2,128,2,64]{1,3,2,0:T(8,128)S(1)}, ...), condition=%wide.region_24.25_spmd, body=%wide.region_19.24_spmd.sunk | while | flops 482347136 | bytes 61189336 | solution.py:233
  895.4 5.7 gather_fusion.8
  949.6 4.8 gather_fusion.11
  961.1 5.7 gather_fusion.8
  1013.9 5.2 copy.184
  1023.8 5.3 copy.185
  1031.5 129.8 %reduce-scatter.15.cloned.1.call-done = f32[128,128]{0,1:T(8,128)} async-done(((f32[8192,128]{0,1:T(8,128)}), f32[128,128]{0,1:T(8,128)}) %reduce-scatter.15.cloned.1.call-update) | async-done | bytes 65552 | tf_op jit(solution)/shard_map/reduce_scatter | solution.py:255
  1162.3 145.3 %reduce-scatter.13.cloned.1.call-done = f32[128,128]{0,1:T(8,128)} async-done(((f32[8192,128]{0,1:T(8,128)}), f32[128,128]{0,1:T(8,128)}) %reduce-scatter.13.cloned.1.call-update) | async-done | bytes 65552 | tf_op jit(solution)/shard_map/reduce_scatter | solution.py:252
  1312.6 20.7 %reduce-scatter.11.cloned.1.call-done = f32[256,128]{1,0:T(8,128)} async-done(((f32[256,512]{1,0:T(8,128)}), f32[256,128]{1,0:T(8,128)}) %reduce-scatter.11.cloned.1.call-update) | async-done | bytes 131088 | tf_op jit(solution)/shard_map/reduce_scatter | solution.py:262
  1334.8 188.6 %all-reduce.5.cloned.1.call-done = f32[4,512,128]{1,2,0:T(8,128)} async-done(((f32[4,512,128]{1,2,0:T(8,128)}), f32[4,512,128]{1,2,0:T(8,128)}) %all-reduce.5.cloned.1.call-update) | async-done | bytes 1048592 | tf_op jit(solution)/shard_map/psum | solution.py:265
  1525.9 20.6 %reduce-scatter.17.cloned.1.call-done = f32[128,128]{1,0:T(8,128)} async-done(((f32[128,512]{1,0:T(8,128)}), f32[128,128]{1,0:T(8,128)}) %reduce-scatter.17.cloned.1.call-update) | async-done | bytes 65552 | tf_op jit(solution)/shard_map/reduce_scatter | solution.py:263
  (261 shorter events, 230.9 us)
Async XLA Ops:
  7.2 27.2 %copy-start = (bf16[512,128]{1,0:T(8,128)(2,1)S(1)}, bf16[512,128]{1,0:T(8,128)(2,1)}, u32[]{:S(2)}) copy-start(bf16[512,128]{1,0:T(8,128)(2,1)} %param.18) | copy-start | bytes 393220
  7.2 92.2 %all-gather.5.cloned.1.call-start = ((), (), s32[]{:S(2)}) async-start(), calls=%async_computation.6 | async-start | bytes 2129920 | tf_op jit(solution)/shard_map/all_gather | solution.py:51
  19.0 15.3 copy-start.8
  20.8 156.9 %all-gather.7.cloned.1.call-start = ((), (), s32[]{:S(2)}) async-start(), calls=%async_computation.7 | async-start | bytes 2129920 | tf_op jit(solution)/shard_map/all_gather | solution.py:52
  22.6 325.3 %all-reduce.3.cloned.1.call-start = ((), (), s32[]{:S(2)}) async-start(), calls=%async_computation.8 | async-start | bytes 131072 | tf_op jit(solution)/shard_map/pmax | solution.py:92
  34.3 97.2 %copy-start.6 = (bf16[256,512]{1,0:T(8,128)(2,1)}, bf16[256,512]{1,0:T(8,128)(2,1)S(1)}, u32[]{:S(2)}) copy-start(bf16[256,512]{1,0:T(8,128)(2,1)S(1)} %all_gather.18) | copy-start | bytes 786436
  34.7 72.9 %copy-start.22 = (s32[32,2]{0,1:T(2,128)S(1)}, s32[32,2]{0,1:T(2,128)}, u32[]{:S(2)}) copy-start(s32[32,2]{0,1:T(2,128)} %param.24) | copy-start | bytes 772
  107.6 24.0 %copy-start.13 = (bf16[512,128]{1,0:T(8,128)(2,1)S(1)}, bf16[512,128]{1,0:T(8,128)(2,1)}, u32[]{:S(2)}) copy-start(bf16[512,128]{1,0:T(8,128)(2,1)} %param.19) | copy-start | bytes 393220
  131.5 429.8 %reduce-scatter.19.cloned.1.call-start = ((), (), s32[]{:S(2)}) async-start(), calls=%async_computation.17 | async-start | bytes 4259840
  376.7 3.9 copy-start.1
  410.1 3.9 copy-start.1
  420.5 286.9 %reduce-scatter.9.cloned.1.call-start = ((), (), s32[]{:S(2)}) async-start(), calls=%async_computation.9 | async-start | bytes 4259840 | tf_op jit(solution)/shard_map/reduce_scatter | solution.py:139
  430.4 279.3 %copy-start.20 = (bf16[256,128]{1,0:T(8,128)(2,1)S(1)}, bf16[256,128]{1,0:T(8,128)(2,1)}, u32[]{:S(2)}) copy-start(bf16[256,128]{1,0:T(8,128)(2,1)} %param.22) | copy-start | bytes 196612
  430.5 351.9 %all-gather.9.cloned.1.call-start = ((), (), s32[]{:S(2)}) async-start(), calls=%async_computation.10 | async-start | bytes 2129920 | tf_op jit(solution)/shard_map/all_gather | solution.py:153
  708.9 148.3 %all-gather.11.cloned.1.call-start = ((), (), s32[]{:S(2)}) async-start(), calls=%async_computation.11 | async-start | bytes 2129920 | tf_op jit(solution)/shard_map/all_gather | solution.py:154
  709.7 451.6 %reduce-scatter.15.cloned.1.call-start = ((), (), s32[]{:S(2)}) async-start(), calls=%async_computation.14 | async-start | bytes 4259840 | tf_op jit(solution)/shard_map/reduce_scatter | solution.py:255
  710.0 149.9 %copy-start.11 = (bf16[2,128,2,64]{1,0,3,2:T(2,128)(2,1)}, bf16[2,128,2,64]{1,0,3,2:T(2,128)(2,1)S(1)}, u32[]{:S(2)}) copy-start(bf16[2,128,2,64]{1,0,3,2:T(2,128)(2,1)S(1)} %copy.104) | copy-start | bytes 196612
  933.9 2.6 copy-start.2
  933.9 2.6 copy-start.24
  936.5 3.4 copy-start.5
  999.6 2.6 copy-start.2
  999.6 2.6 copy-start.24
  1002.2 3.4 copy-start.5
  1019.1 288.5 %reduce-scatter.13.cloned.1.call-start = ((), (), s32[]{:S(2)}) async-start(), calls=%async_computation.13 | async-start | bytes 4259840 | tf_op jit(solution)/shard_map/reduce_scatter | solution.py:252
  1029.1 304.2 %reduce-scatter.11.cloned.1.call-start = ((), (), s32[]{:S(2)}) async-start(), calls=%async_computation.12 | async-start | bytes 655360 | tf_op jit(solution)/shard_map/reduce_scatter | solution.py:262
  1029.1 132.1 %copy-start.9 = (bf16[128,512]{1,0:T(8,128)(2,1)S(1)}, bf16[128,512]{1,0:T(8,128)(2,1)}, u32[]{:S(2)}) copy-start(bf16[128,512]{1,0:T(8,128)(2,1)} %copy-done.8) | copy-start | bytes 393220
  1031.0 492.3 %all-reduce.5.cloned.1.call-start = ((), (), s32[]{:S(2)}) async-start(), calls=%async_computation.16 | async-start | bytes 2097152 | tf_op jit(solution)/shard_map/psum | solution.py:265
  1031.5 278.4 %copy-start.15 = (bf16[512,128]{1,0:T(8,128)(2,1)S(1)}, bf16[512,128]{1,0:T(8,128)(2,1)}, u32[]{:S(2)}) copy-start(bf16[512,128]{1,0:T(8,128)(2,1)} %param.20) | copy-start | bytes 393220
  1162.3 147.8 %copy-start.16 = (bf16[512,128]{1,0:T(8,128)(2,1)S(1)}, bf16[512,128]{1,0:T(8,128)(2,1)}, u32[]{:S(2)}) copy-start(bf16[512,128]{1,0:T(8,128)(2,1)} %param.21) | copy-start | bytes 393220
  1162.3 147.8 %copy-start.21 = (f32[128,128]{0,1:T(8,128)S(1)}, f32[128,128]{0,1:T(8,128)}, u32[]{:S(2)}) copy-start(f32[128,128]{0,1:T(8,128)} %reduce-scatter.15.cloned.1.call-done) | copy-start | bytes 196612
  1308.7 3.1 copy-start.18
  1309.8 236.7 %reduce-scatter.17.cloned.1.call-start = ((), (), s32[]{:S(2)}) async-start(), calls=%async_computation.15 | async-start | bytes 327680 | tf_op jit(solution)/shard_map/reduce_scatter | solution.py:263
  (20 other events, 25.4 us)
Sparse Core Ops, SparseCore 0:
  20.9 78.4 all-gather.4
  102.7 74.9 all-gather.6
  181.8 166.0 all-reduce.2
  420.7 140.5 reduce-scatter.18
  565.3 142.0 reduce-scatter.8
  710.7 71.6 all-gather.8
  785.8 71.3 all-gather.10
  1019.2 141.9 reduce-scatter.14
  1165.4 142.1 reduce-scatter.12
  1310.2 23.0 reduce-scatter.10
  1337.7 185.6 all-reduce.4
  1525.7 20.7 reduce-scatter.16
where the time goes:
time: 1570 us; the launch traced here: 1560 us
  waiting for transfers between devices  1200 us (76%)
  local copies, waits for them, and re-layouts  209 us (13%)
  other arithmetic  58.9 us (4%)
  matrix products  46.7 us (3%)
  blocking collectives  23.5 us (1%)
    psum x1, waiting for transfers between devices, body(): lax.psum(jnp.stack([weight_rf, weight_vf, weight_rm, weight_vm]), 'fluid')  189 us
    pmax x1, waiting for transfers between devices, body(): col_max = lax.pmax(col_local, 'fluid')  162 us
    reduce_scatter x1, waiting for transfers between devices, body(): lax.psum_scatter(grad_rm.reshape(metal_rows, feature_cols), 'fluid', scat...  145 us
    reduce_scatter x1, waiting for transfers between devices, body(): lax.psum_scatter(num_rows, 'fluid', scatter_dimension=0, tiled=True)  145 us
    unnamed x13, waiting for transfers between devices  131 us
    reduce_scatter x1, waiting for transfers between devices, body(): lax.psum_scatter(grad_vm.reshape(metal_rows, feature_cols), 'fluid', scat...  130 us
    all_gather x1, waiting for transfers between devices, body(): lax.all_gather(metal_out, 'fluid', axis=0, tiled=True)  74.9 us
    all_gather x1, waiting for transfers between devices, body(): lax.all_gather(scaled_grad, 'fluid', axis=0, tiled=True)  72.3 us
  transfers between devices with their start and end apart: 12, of which 12 were waited for; matrix products, arithmetic and copies ran while one was open for 5% of the time, Pallas kernels for 0%

commit v1 on v0

--- a/solution.py
+++ b/solution.py
@@ -262,7 +262,8 @@
         lax.psum_scatter(fluid_part, "metal", scatter_dimension=1, tiled=True),
         lax.psum_scatter(metal_part, "metal", scatter_dimension=1, tiled=True),
     )
-    weight_grads = lax.psum(jnp.stack([weight_rf, weight_vf, weight_rm, weight_vm]), "fluid")
+    t0 = jnp.stack([weight_rf, weight_vf, weight_rm, weight_vm])
+    weight_grads = jnp.sum(lax.all_gather(t0, "fluid"), 0)
     return (
         fluid_out,
         metal_out,

time: 1570 us -> 1640 us (1.045)
  waiting for transfers between devices: 1200 us -> 1240 us
  other arithmetic: 58.9 us -> 83 us
    all_gather x0 -> x1, waiting for transfers between devices: none -> 237 us  [body(): weight_grads = jnp.sum(lax.all_gather(t0, 'fluid'), 0)]
    psum x1 -> x0, waiting for transfers between devices: 189 us -> none  [body(): lax.psum(jnp.stack([weight_rf, weight_vf, weight_rm, weight_vm]), 'fluid')]
    reduce_sum x0 -> x1, other arithmetic: none -> 21.7 us  [body(): weight_grads = jnp.sum(lax.all_gather(t0, 'fluid'), 0)]
where the time goes in v1:
time: 1640 us; the launch traced here: 1630 us
  waiting for transfers between devices  1240 us (76%)
  local copies, waits for them, and re-layouts  197 us (12%)
  other arithmetic  83 us (5%)
  matrix products  62.6 us (4%)
  blocking collectives  23.5 us (1%)
    all_gather x1, waiting for transfers between devices, body(): weight_grads = jnp.sum(lax.all_gather(t0, 'fluid'), 0)  237 us
    pmax x1, waiting for transfers between devices, body(): col_max = lax.pmax(col_local, 'fluid')  162 us
    reduce_scatter x1, waiting for transfers between devices, body(): lax.psum_scatter(num_rows, 'fluid', scatter_dimension=0, tiled=True)  145 us
    reduce_scatter x1, waiting for transfers between devices, body(): lax.psum_scatter(grad_vm.reshape(metal_rows, feature_cols), 'fluid', scat...  145 us
    unnamed x13, waiting for transfers between devices  131 us
    reduce_scatter x1, waiting for transfers between devices, body(): lax.psum_scatter(grad_rm.reshape(metal_rows, feature_cols), 'fluid', scat...  130 us
    all_gather x1, waiting for transfers between devices, body(): lax.all_gather(scaled_grad, 'fluid', axis=0, tiled=True)  72.3 us
    all_gather x1, waiting for transfers between devices, body(): lax.all_gather(metal_out, 'fluid', axis=0, tiled=True)  67.5 us
  transfers between devices with their start and end apart: 12, of which 12 were waited for; matrix products, arithmetic and copies ran while one was open for 5% of the time, Pallas kernels for 0%

profile of v1, /device:TPU:2, one launch (start us, length us, event | category | flops | bytes accessed | tf_op | source)
XLA Modules:
  0.0 1627.5 jit_solution(9833254035275752713)
XLA Ops:
  7.2 11.8 all_gather.25
  22.6 11.7 all_gather.24
  34.7 64.7 %all-gather.7.cloned.1.call-done = bf16[8192,128]{1,0:T(8,128)(2,1)} async-done(((bf16[128,128]{1,0:T(8,128)(2,1)}), bf16[8192,128]{1,0:T(8,128)(2,1)}) %all-gather.7.cloned.1.call-update) | async-done | bytes 2097168 | tf_op jit(solution)/shard_map/all_gather | solution.py:51
  99.4 8.2 reshape.335
  107.6 23.2 %while.53 = (s32[]{:T(128)}, f32[2,2,128]{2,1,0:T(2,128)S(1)}, f32[64,2,128]{2,1,0:T(2,128)S(1)}, s32[32,2]{0,1:T(2,128)S(1)}, s32[]{:T(128)}, /*index=5*/bf16[2...) while((s32[]{:T(128)}, f32[2,2,128]{2,1,0:T(2,128)S(1)}, ...), condition=%wide.region_5.6_spmd, body=%wide.region_0.5_spmd.sunk | while | flops 68692104 | bytes 3351631 | solution.py:83
  119.3 4.8 gather_fusion
  131.9 45.8 %all-gather.9.cloned.1.call-done = bf16[8192,128]{1,0:T(8,128)(2,1)} async-done(((bf16[128,128]{1,0:T(8,128)(2,1)}), bf16[8192,128]{1,0:T(8,128)(2,1)}) %all-gather.9.cloned.1.call-update) | async-done | bytes 2097168 | tf_op jit(solution)/shard_map/all_gather | solution.py:52
  177.7 8.3 reshape.336
  186.0 161.9 %all-reduce.2.cloned.1.call-done = f32[64,2,128]{2,1,0:T(2,128)} async-done(((f32[64,2,128]{2,1,0:T(2,128)}), f32[64,2,128]{2,1,0:T(2,128)}) %all-reduce.2.cloned.1.call-update) | async-done | bytes 65552 | tf_op jit(solution)/shard_map/pmax | solution.py:92
  350.4 79.8 %while.54 = (s32[]{:T(128)}, f32[2,2,128]{2,1,0:T(2,128)S(1)}, f32[2,128,2,64]{1,3,2,0:T(8,128)S(1)}, f32[64,2,128]{2,1,0:T(2,128)S(1)}, f32[64,128,2,64]{1,3,2,...) while((s32[]{:T(128)}, f32[2,2,128]{2,1,0:T(2,128)S(1)}, ...), condition=%wide.region_14.15_spmd, body=%wide.region_7.14_spmd.sunk | while | flops 209717376 | bytes 21243424 | solution.py:120
  353.3 5.7 gather_fusion.4
  367.0 5.7 gather_fusion.6
  392.9 5.7 gather_fusion.4
  406.6 5.7 gather_fusion.6
  437.5 5.2 copy.187
  443.6 130.1 %reduce-scatter.19.cloned.1.call-done = f32[128,2]{1,0:T(8,128)} async-done(((f32[8192,2]{1,0:T(8,128)}), f32[128,2]{1,0:T(8,128)}) %reduce-scatter.19.cloned.1.call-update) | async-done | bytes 1040
  574.5 145.3 %reduce-scatter.9.cloned.1.call-done = f32[128,128]{0,1:T(8,128)} async-done(((f32[8192,128]{0,1:T(8,128)}), f32[128,128]{0,1:T(8,128)}) %reduce-scatter.9.cloned.1.call-update) | async-done | bytes 65552 | tf_op jit(solution)/shard_map/reduce_scatter | solution.py:139
  722.5 72.3 %all-gather.11.cloned.1.call-done = bf16[8192,128]{0,1:T(8,128)(2,1)} async-done(((bf16[128,128]{0,1:T(8,128)(2,1)}), bf16[8192,128]{0,1:T(8,128)(2,1)}) %all-gather.11.cloned.1.call-update) | async-done | bytes 2097168 | tf_op jit(solution)/shard_map/all_gather | solution.py:153
  797.0 5.2 copy.112
  802.1 67.5 %all-gather.13.cloned.1.call-done = bf16[8192,128]{0,1:T(8,128)(2,1)} async-done(((bf16[128,128]{0,1:T(8,128)(2,1)}), bf16[8192,128]{0,1:T(8,128)(2,1)}) %all-gather.13.cloned.1.call-update) | async-done | bytes 2097168 | tf_op jit(solution)/shard_map/all_gather | solution.py:154
  882.5 128.4 %while.55 = (s32[]{:T(128)}, f32[2,128,2,64]{1,3,2,0:T(8,128)S(1)}, f32[2,128,2,64]{1,3,2,0:T(8,128)S(1)}, f32[64,128,2,64]{1,3,2,0:T(8,128)}, f32[64,128,2,64]{...) while((s32[]{:T(128)}, f32[2,128,2,64]{1,3,2,0:T(8,128)S(1)}, ...), condition=%wide.region_24.25_spmd, body=%wide.region_19.24_spmd.sunk | while | flops 482347136 | bytes 61191380 | solution.py:233
  882.8 4.8 gather_fusion.8
  891.7 5.0 gather_fusion.10
  955.8 5.0 gather_fusion.10
  1015.6 5.2 copy.186
  1025.5 5.3 copy.185
  1032.8 130.1 %reduce-scatter.13.cloned.1.call-done = f32[128,128]{0,1:T(8,128)} async-done(((f32[8192,128]{0,1:T(8,128)}), f32[128,128]{0,1:T(8,128)}) %reduce-scatter.13.cloned.1.call-update) | async-done | bytes 65552 | tf_op jit(solution)/shard_map/reduce_scatter | solution.py:252
  1164.0 145.1 %reduce-scatter.15.cloned.1.call-done = f32[128,128]{0,1:T(8,128)} async-done(((f32[8192,128]{0,1:T(8,128)}), f32[128,128]{0,1:T(8,128)}) %reduce-scatter.15.cloned.1.call-update) | async-done | bytes 65552 | tf_op jit(solution)/shard_map/reduce_scatter | solution.py:255
  1314.8 20.2 %reduce-scatter.11.cloned.1.call-done = f32[256,128]{1,0:T(8,128)} async-done(((f32[256,512]{1,0:T(8,128)}), f32[256,128]{1,0:T(8,128)}) %reduce-scatter.11.cloned.1.call-update) | async-done | bytes 131088 | tf_op jit(solution)/shard_map/reduce_scatter | solution.py:262
  1336.5 24.0 %reduce-scatter.17.cloned.1.call-done = f32[128,128]{1,0:T(8,128)} async-done(((f32[128,512]{1,0:T(8,128)}), f32[128,128]{1,0:T(8,128)}) %reduce-scatter.17.cloned.1.call-update) | async-done | bytes 65552 | tf_op jit(solution)/shard_map/reduce_scatter | solution.py:263
  1362.0 236.6 %all-gather.15.cloned.1.call-done = f32[256,512,128]{2,1,0:T(8,128)} async-done(((f32[4,512,128]{2,1,0:T(8,128)}), f32[256,512,128]{2,1,0:T(8,128)}) %all-gather.15.cloned.1.call-update) | async-done | bytes 67108880 | tf_op jit(solution)/shard_map/all_gather | solution.py:266
  1598.6 21.7 %reduce_sum.55 = f32[4,512,128]{2,1,0:T(8,128)} reduce(f32[64,4,512,128]{3,2,1,0:T(8,128)} %bitcast.29, f32[]{:T(128)} %constant.175.clone.1), dimensions={0}, to_apply=%region_29.30 | reduce | flops 16515072 | bytes 68157440 | tf_op jit(solution)/shard_map/reduce_sum | solution.py:266
  (266 shorter events, 242.0 us)
Async XLA Ops:
  7.2 27.2 %copy-start = (bf16[512,128]{1,0:T(8,128)(2,1)S(1)}, bf16[512,128]{1,0:T(8,128)(2,1)}, u32[]{:S(2)}) copy-start(bf16[512,128]{1,0:T(8,128)(2,1)} %param.18) | copy-start | bytes 393220
  7.2 92.2 %all-gather.7.cloned.1.call-start = ((), (), s32[]{:S(2)}) async-start(), calls=%async_computation.6 | async-start | bytes 2129920 | tf_op jit(solution)/shard_map/all_gather | solution.py:51
  19.0 15.3 copy-start.8
  20.8 156.9 %all-gather.9.cloned.1.call-start = ((), (), s32[]{:S(2)}) async-start(), calls=%async_computation.7 | async-start | bytes 2129920 | tf_op jit(solution)/shard_map/all_gather | solution.py:52
  22.6 325.3 %all-reduce.2.cloned.1.call-start = ((), (), s32[]{:S(2)}) async-start(), calls=%async_computation.8 | async-start | bytes 131072 | tf_op jit(solution)/shard_map/pmax | solution.py:92
  34.3 97.2 %copy-start.6 = (bf16[256,512]{1,0:T(8,128)(2,1)}, bf16[256,512]{1,0:T(8,128)(2,1)S(1)}, u32[]{:S(2)}) copy-start(bf16[256,512]{1,0:T(8,128)(2,1)S(1)} %all_gather.24) | copy-start | bytes 786436
  34.7 72.9 %copy-start.22 = (s32[32,2]{0,1:T(2,128)S(1)}, s32[32,2]{0,1:T(2,128)}, u32[]{:S(2)}) copy-start(s32[32,2]{0,1:T(2,128)} %param.24) | copy-start | bytes 772
  107.6 23.9 %copy-start.13 = (bf16[512,128]{1,0:T(8,128)(2,1)S(1)}, bf16[512,128]{1,0:T(8,128)(2,1)}, u32[]{:S(2)}) copy-start(bf16[512,128]{1,0:T(8,128)(2,1)} %param.19) | copy-start | bytes 393220
  131.5 442.1 %reduce-scatter.19.cloned.1.call-start = ((), (), s32[]{:S(2)}) async-start(), calls=%async_computation.17 | async-start | bytes 4259840
  432.8 287.0 %reduce-scatter.9.cloned.1.call-start = ((), (), s32[]{:S(2)}) async-start(), calls=%async_computation.9 | async-start | bytes 4259840 | tf_op jit(solution)/shard_map/reduce_scatter | solution.py:139
  442.7 279.4 %copy-start.20 = (bf16[256,128]{1,0:T(8,128)(2,1)S(1)}, bf16[256,128]{1,0:T(8,128)(2,1)}, u32[]{:S(2)}) copy-start(bf16[256,128]{1,0:T(8,128)(2,1)} %param.22) | copy-start | bytes 196612
  442.7 352.1 %all-gather.11.cloned.1.call-start = ((), (), s32[]{:S(2)}) async-start(), calls=%async_computation.10 | async-start | bytes 2129920 | tf_op jit(solution)/shard_map/all_gather | solution.py:153
  721.3 148.4 %all-gather.13.cloned.1.call-start = ((), (), s32[]{:S(2)}) async-start(), calls=%async_computation.11 | async-start | bytes 2129920 | tf_op jit(solution)/shard_map/all_gather | solution.py:154
  722.0 440.9 %reduce-scatter.13.cloned.1.call-start = ((), (), s32[]{:S(2)}) async-start(), calls=%async_computation.13 | async-start | bytes 4259840 | tf_op jit(solution)/shard_map/reduce_scatter | solution.py:252
  722.4 72.4 %copy-start.11 = (bf16[2,128,2,64]{1,0,3,2:T(2,128)(2,1)}, bf16[2,128,2,64]{1,0,3,2:T(2,128)(2,1)S(1)}, u32[]{:S(2)}) copy-start(bf16[2,128,2,64]{1,0,3,2:T(2,128)(2,1)S(1)} %copy.102) | copy-start | bytes 196612
  882.7 5.7 copy-start.23
  882.8 8.2 copy-start.25
  882.8 8.2 copy-start.27
  891.7 7.3 copy-start.3
  946.7 5.6 copy-start.23
  946.8 8.2 copy-start.25
  946.8 8.2 copy-start.27
  955.8 7.3 copy-start.3
  1020.8 288.4 %reduce-scatter.15.cloned.1.call-start = ((), (), s32[]{:S(2)}) async-start(), calls=%async_computation.14 | async-start | bytes 4259840 | tf_op jit(solution)/shard_map/reduce_scatter | solution.py:255
  1030.8 132.1 %copy-start.15 = (bf16[512,128]{1,0:T(8,128)(2,1)S(1)}, bf16[512,128]{1,0:T(8,128)(2,1)}, u32[]{:S(2)}) copy-start(bf16[512,128]{1,0:T(8,128)(2,1)} %param.20) | copy-start | bytes 393220
  1030.8 278.4 %copy-start.16 = (bf16[512,128]{1,0:T(8,128)(2,1)S(1)}, bf16[512,128]{1,0:T(8,128)(2,1)}, u32[]{:S(2)}) copy-start(bf16[512,128]{1,0:T(8,128)(2,1)} %param.21) | copy-start | bytes 393220
  1030.8 304.2 %reduce-scatter.11.cloned.1.call-start = ((), (), s32[]{:S(2)}) async-start(), calls=%async_computation.12 | async-start | bytes 655360 | tf_op jit(solution)/shard_map/reduce_scatter | solution.py:262
  1030.9 280.2 %copy-start.7 = (bf16[256,512]{1,0:T(8,128)(2,1)S(1)}, bf16[256,512]{1,0:T(8,128)(2,1)}, u32[]{:S(2)}) copy-start(bf16[256,512]{1,0:T(8,128)(2,1)} %copy-done.6) | copy-start | bytes 786436
  1031.6 279.9 %copy-start.9 = (bf16[128,512]{1,0:T(8,128)(2,1)S(1)}, bf16[128,512]{1,0:T(8,128)(2,1)}, u32[]{:S(2)}) copy-start(bf16[128,512]{1,0:T(8,128)(2,1)} %copy-done.8) | copy-start | bytes 393220
  1032.7 327.8 %reduce-scatter.17.cloned.1.call-start = ((), (), s32[]{:S(2)}) async-start(), calls=%async_computation.15 | async-start | bytes 327680 | tf_op jit(solution)/shard_map/reduce_scatter | solution.py:263
  1162.9 148.8 %copy-start.19 = (f32[128,128]{0,1:T(8,128)S(1)}, f32[128,128]{0,1:T(8,128)}, u32[]{:S(2)}) copy-start(f32[128,128]{0,1:T(8,128)} %reduce-scatter.13.cloned.1.call-done) | copy-start | bytes 196612
  1311.1 287.5 %all-gather.15.cloned.1.call-start = ((), (), s32[]{:S(2)}) async-start(), calls=%async_computation.16 | async-start | bytes 68157440 | tf_op jit(solution)/shard_map/all_gather | solution.py:266
  (22 other events, 52.3 us)
Sparse Core Ops, SparseCore 0:
  20.9 78.4 all-gather.6
  102.7 74.9 all-gather.8
  181.8 166.0 all-reduce.1
  432.9 140.6 reduce-scatter.18
  577.6 142.1 reduce-scatter.8
  723.1 71.6 all-gather.10
  798.2 71.3 all-gather.12
  1020.9 141.9 reduce-scatter.12
  1167.0 142.0 reduce-scatter.14
  1311.7 23.1 reduce-scatter.10
  1337.6 22.8 reduce-scatter.16
  1363.8 234.7 all-gather.14
